TPU v7x, 512 devices: a whole 4x8x8 slice. The times are simulated.
512 devices in a mesh: blk: 64 (over y, x, core), tp: 8 (over z).
Axes of the slice: x: 4, y: 8, z: 8, core: 2. Of those that a mesh axis runs over, the one named last changes fastest.
Arguments:
- inputs: bfloat16 [8192, 8192], P('blk', 'tp'), may hold values from -6 to 6
- grad_out: bfloat16 [8192, 8192], P('blk', 'tp'), may hold values from -6 to 6
- w_up: bfloat16 [128, 2, 128, 128], P('blk'), may hold values from -0.4375 to 0.4375
- w_down: bfloat16 [128, 2, 128, 128], P('blk'), may hold values from -0.3125 to 0.3125
- up_rows: int32 [128, 2], P('blk'), may hold values from 0 to 63, as said below
- slot_counts: int32 [128], P('blk'), may hold values from 1 to 2
- keep_mask: int32 [8192, 1024], P(None, 'blk'), may hold values from 0 to 65535, as said below
Outputs:
- outputs: bfloat16 [8192, 8192], P('blk', 'tp')
- grad_in: bfloat16 [8192, 8192], P('blk', 'tp')
- grad_up: bfloat16 [128, 2, 128, 128], P('blk', None, 'tp')
- grad_down: bfloat16 [128, 2, 128, 128], P('blk', None, 'tp')
Inputs may be any that keep to these rules, and one draw needn't show every extreme that they name: `up_rows`: within each hidden column block, the 2 entries are distinct. `keep_mask`: bit k of word w holds the keep flag of hidden unit 16 w + k.
All inputs are finite; a program needn't handle non-finite values.
Results may differ from a plain program's by a relative error of at most 0.005.
Values may be sent and summed in bfloat16 or wider, within the bound.
A program may use at most 64 MiB of HBM per device.

v0:
```python
import jax
import jax.numpy as jnp
from jax import lax
from jax.sharding import PartitionSpec as P

INV_ROOT_TWO = 0.7071067811865476
INV_ROOT_TAU = 0.3989422804014327
KEEP_SCALE = 1.25


def gelu_value(value):
    return 0.5 * value * (1.0 + jax.scipy.special.erf(value * INV_ROOT_TWO))


def gelu_slope(value):
    return (
        0.5 * (1.0 + jax.scipy.special.erf(value * INV_ROOT_TWO))
        + value * jnp.exp(-0.5 * value * value) * INV_ROOT_TAU
    )


def combine_terms(received, flat_owner, part_rows, row_blocks, tile):
    selector = (flat_owner[:, None] == jnp.arange(row_blocks, dtype=jnp.int32)[None, :]).astype(
        jnp.float32
    )
    stacked = received.reshape(part_rows, flat_owner.shape[0], tile)
    summed = jnp.einsum("nsl,sr->nrl", stacked, selector, precision=lax.Precision.HIGHEST)
    return summed.reshape(part_rows, row_blocks * tile).astype(jnp.bfloat16)


def per_device(inputs, grad_out, w_up, w_down, up_rows, slot_counts, keep_mask):
    tok_dev, width_local = inputs.shape
    col_local, slots, tile, _unused = w_up.shape
    parts = lax.axis_size("tp")
    blocks = lax.axis_size("blk")
    width = width_local * parts
    row_blocks = width // tile
    part_rows = tok_dev // parts
    held = part_rows * blocks
    span = col_local * slots
    live = jnp.arange(slots, dtype=jnp.int32)[None, :] < slot_counts[:, None]
    live_tiles = live[:, :, None, None]
    up_live = jnp.where(live_tiles, w_up, jnp.zeros((), jnp.bfloat16))
    down_live = jnp.where(live_tiles, w_down, jnp.zeros((), jnp.bfloat16))
    owner_rows = lax.all_gather(up_rows, "blk", axis=0, tiled=True)
    flat_owner = owner_rows.reshape(-1)

    def select_tiles(rows_full):
        blocked = rows_full.reshape(part_rows, row_blocks, tile)
        return jnp.take(blocked, flat_owner, axis=1).reshape(part_rows, blocks, span * tile)

    def as_tiles(received):
        return received.reshape(held, col_local, slots, tile)

    def combine(received):
        return combine_terms(received, flat_owner, part_rows, row_blocks, tile)

    in_rows, out_rows = (
        lax.all_to_all(inputs, "tp", split_axis=0, concat_axis=1, tiled=True),
        lax.all_to_all(grad_out, "tp", split_axis=0, concat_axis=1, tiled=True),
    )
    recv_in, recv_out = (
        lax.all_to_all(select_tiles(in_rows), "blk", split_axis=1, concat_axis=0, tiled=True),
        lax.all_to_all(select_tiles(out_rows), "blk", split_axis=1, concat_axis=0, tiled=True),
    )
    input_tiles = as_tiles(recv_in)
    cotangent_tiles = as_tiles(recv_out)
    word_count = keep_mask.shape[1]
    words = keep_mask.reshape(blocks, parts, part_rows, word_count)
    mine = lax.dynamic_index_in_dim(words, lax.axis_index("tp"), 1, keepdims=False).reshape(
        held, word_count
    )
    columns = jnp.arange(col_local * tile, dtype=jnp.int32)
    picked = jnp.take(mine, columns // 16, axis=1)
    keep = jnp.bitwise_and(jnp.right_shift(picked, columns % 16), 1)
    scale = keep.astype(jnp.float32) * KEEP_SCALE
    pre = jnp.einsum(
        "nckp,ckpj->ncj", input_tiles, up_live, preferred_element_type=jnp.float32
    ).reshape(held, col_local * tile)
    hidden = (gelu_value(pre) * scale).astype(jnp.bfloat16)
    hidden_blocks = hidden.reshape(held, col_local, tile)
    out_part = jnp.einsum(
        "ncj,ckjl->nckl", hidden_blocks, down_live, preferred_element_type=jnp.float32
    ).reshape(held, span * tile)
    out_recv = lax.all_to_all(out_part, "blk", split_axis=0, concat_axis=1, tiled=True)
    outputs = lax.all_to_all(combine(out_recv), "tp", split_axis=1, concat_axis=0, tiled=True)
    grad_hidden = jnp.einsum(
        "nckl,ckjl->ncj", cotangent_tiles, down_live, preferred_element_type=jnp.float32
    ).reshape(held, col_local * tile)
    grad_pre = (grad_hidden * scale * gelu_slope(pre)).astype(jnp.bfloat16)
    grad_blocks = grad_pre.reshape(held, col_local, tile)
    in_part = jnp.einsum(
        "ncj,ckpj->nckp", grad_blocks, up_live, preferred_element_type=jnp.float32
    ).reshape(held, span * tile)
    in_recv = lax.all_to_all(in_part, "blk", split_axis=0, concat_axis=1, tiled=True)
    grad_in = lax.all_to_all(combine(in_recv), "tp", split_axis=1, concat_axis=0, tiled=True)
    up_sum = jnp.einsum(
        "nckp,ncj->ckpj", input_tiles, grad_blocks, preferred_element_type=jnp.float32
    )
    down_sum = jnp.einsum(
        "ncj,nckl->ckjl", hidden_blocks, cotangent_tiles, preferred_element_type=jnp.float32
    )
    up_share, down_share = (
        lax.psum_scatter(up_sum, "tp", scatter_dimension=2, tiled=True),
        lax.psum_scatter(down_sum, "tp", scatter_dimension=2, tiled=True),
    )
    grad_up = jnp.where(live_tiles, up_share, 0.0).astype(jnp.bfloat16)
    grad_down = jnp.where(live_tiles, down_share, 0.0).astype(jnp.bfloat16)
    return (outputs, grad_in, grad_up, grad_down)


def solution(mesh):
    return jax.shard_map(
        per_device,
        mesh=mesh,
        in_specs=(
            P("blk", "tp"),
            P("blk", "tp"),
            P("blk", None, None, None),
            P("blk", None, None, None),
            P("blk", None),
            P("blk"),
            P(None, "blk"),
        ),
        out_specs=(
            P("blk", "tp"),
            P("blk", "tp"),
            P("blk", None, "tp", None),
            P("blk", None, "tp", None),
        ),
        check_vma=False,
    )
```

profile of v0, /device:TPU:6, one launch (start us, length us, event | category | flops | bytes accessed | tf_op | source)
XLA Modules:
  0.0 339.3 jit_solution(14502978726614844054)
XLA Ops:
  7.2 10.3 %all-to-all-start = ((bf16[8,16,1024]{2,1,0:T(8,128)(2,1)}), bf16[8,16,1024]{2,1,0:T(8,128)(2,1)S(1)}, u32[]{:S(2)}, u32[]{:S(2)}) async-start(bf16[8,16,1024]{2,1,0:T(8,128)(2,1)} %bitcast.100), calls=%async_computation | async-start | bytes 524288 | tf_op jit(solution)/shard_map/all_to_all | solution.py:59
  17.5 38.4 %all-gather = s32[64,2,2]{2,1,0:T(2,128)S(1)} all-gather(s32[1,2,2]{2,1,0:T(2,128)} %bitcast.102), channel_id=1, replica_groups=mesh['blk'=64,'tp'=8] {'blk'}, dimensions={0}, use_global_device_ids=true | all-gather | bytes 1040 | tf_op jit(solution)/shard_map/all_gather | solution.py:45
  56.0 7.2 %all-to-all-start.4 = ((bf16[8,16,1024]{2,1,0:T(8,128)(2,1)}), bf16[8,16,1024]{2,1,0:T(8,128)(2,1)S(1)}, u32[]{:S(2)}, u32[]{:S(2)}) async-start(bf16[8,16,1024]{2,1,0:T(8,128)(2,1)} %bitcast.101), calls=%async_computation.4 | async-start | bytes 524288 | tf_op jit(solution)/shard_map/all_to_all | solution.py:60
  63.3 0.2 copy.50
  63.5 0.2 copy.51
  63.7 12.1 %all-to-all-done.4 = bf16[8,16,1024]{2,1,0:T(8,128)(2,1)S(1)} async-done(((bf16[8,16,1024]{2,1,0:T(8,128)(2,1)}), bf16[8,16,1024]{2,1,0:T(8,128)(2,1)S(1)}, u32[]{:S(2)}, u32[]{:S(2)}) %all-to-all-start.4) | async-done | bytes 262176 | tf_op jit(solution)/shard_map/all_to_all | solution.py:60
  75.8 0.1 copy.61
  76.1 0.2 copy.62
  76.3 0.8 gather_fusion.1
  77.1 0.8 gather_fusion.2
  78.0 0.9 select_bitcast_fusion
  78.9 0.3 copy.52
  79.2 0.7 reshape.186
  79.9 1.6 copy.53
  81.5 8.4 %all-to-all-start.1 = ((bf16[16,64,512]{2,0,1:T(8,128)(2,1)}), bf16[16,64,512]{2,0,1:T(8,128)(2,1)S(1)}, u32[]{:S(2)}, u32[]{:S(2)}) async-start(bf16[16,64,512]{2,0,1:T(8,128)(2,1)} %copy.53), calls=%async_computation.1 | async-start | bytes 2097152 | tf_op jit(solution)/shard_map/all_to_all | solution.py:63
  89.8 0.3 copy.63
  90.1 0.7 reshape.192
  90.8 1.5 copy.64
  92.3 26.3 %all-to-all-done.1 = bf16[16,64,512]{2,0,1:T(8,128)(2,1)S(1)} async-done(((bf16[16,64,512]{2,0,1:T(8,128)(2,1)}), bf16[16,64,512]{2,0,1:T(8,128)(2,1)S(1)}, u32[]{:S(2)}, u32[]{:S(2)}) %all-to-all-start.1) | async-done | bytes 1048608 | tf_op jit(solution)/shard_map/all_to_all | solution.py:63
  118.6 5.8 %all-to-all-start.5 = ((bf16[16,64,512]{2,0,1:T(8,128)(2,1)}), bf16[16,64,512]{2,0,1:T(8,128)(2,1)}, u32[]{:S(2)}, u32[]{:S(2)}) async-start(bf16[16,64,512]{2,0,1:T(8,128)(2,1)} %copy.64), calls=%async_computation.5 | async-start | bytes 2097152 | tf_op jit(solution)/shard_map/all_to_all | solution.py:64
  124.5 2.8 reshape.188
  127.3 3.7 %dynamic-slice_reduce_fusion = s32[64,16,16]{1,0,2:T(8,128)S(1)} fusion(s32[64,8,16,16]{2,1,0,3:T(8,128)} %reshape.188, s32[]{:T(128)S(6)} %select_n.78), kind=kLoop, calls=%fused_computation.27 | loop fusion | bytes 131076 | tf_op jit(solution)/shard_map/jit(dynamic_index_in_dim)/dynamic_slice | solution.py:70
  131.0 0.3 reshape.189
  131.3 1.1 gather_fusion
  132.5 1.2 reshape.187
  133.7 2.4 copy.70
  136.2 17.0 %all-to-all-done.5 = bf16[16,64,512]{2,0,1:T(8,128)(2,1)} async-done(((bf16[16,64,512]{2,0,1:T(8,128)(2,1)}), bf16[16,64,512]{2,0,1:T(8,128)(2,1)}, u32[]{:S(2)}, u32[]{:S(2)}) %all-to-all-start.5) | async-done | bytes 1048608 | tf_op jit(solution)/shard_map/all_to_all | solution.py:64
  153.2 2.2 reshape.193
  155.4 3.7 %copy.72 = bf16[1024,2,2,128]{0,3,2,1:T(8,128)(2,1)} copy(bf16[1024,2,2,128]{3,2,1,0:T(2,128)(2,1)} %reshape.193) | data formatting | bytes 2097152 | tf_op jit(solution)/shard_map/reshape | solution.py:53
  159.1 0.4 convolution_bitcast_fusion.3
  159.6 0.8 copy-done.4
  160.4 0.8 fusion.3
  161.2 0.9 copy-done.6
  162.1 1.8 convolution_bitcast_fusion
  163.9 3.1 copy.67
  167.0 2.7 all_to_all.112
  169.7 5.6 %all-to-all-start.6 = ((f32[64,16,512]{2,1,0:T(8,128)}), f32[64,16,512]{2,1,0:T(8,128)S(1)}, u32[]{:S(2)}, u32[]{:S(2)}) async-start(f32[64,16,512]{2,1,0:T(8,128)} %all_to_all.112), calls=%async_computation.6 | async-start | bytes 4194304 | tf_op jit(solution)/shard_map/all_to_all | solution.py:95
  175.3 2.0 fusion.10
  177.3 0.8 copy-done.1
  178.1 1.9 convolution_bitcast_fusion.1
  179.9 4.1 %copy.58 = f32[1024,2,2,128]{3,2,1,0:T(2,128)} copy(f32[1024,2,2,128]{0,3,2,1:T(8,128)} %convolution_bitcast_fusion.1) | data formatting | bytes 4194304 | tf_op jit(solution)/shard_map/ncj,ckjl->nckl/transpose | solution.py:82
  184.1 3.9 %all_to_all.100 = f32[64,16,512]{2,1,0:T(8,128)} reshape(f32[1024,2,2,128]{3,2,1,0:T(2,128)} %copy.58) | data formatting | bytes 4194304 | tf_op jit(solution)/shard_map/all_to_all | solution.py:85
  187.9 38.6 %all-to-all-done.6 = f32[64,16,512]{2,1,0:T(8,128)S(1)} async-done(((f32[64,16,512]{2,1,0:T(8,128)}), f32[64,16,512]{2,1,0:T(8,128)S(1)}, u32[]{:S(2)}, u32[]{:S(2)}) %all-to-all-start.6) | async-done | bytes 2097184 | tf_op jit(solution)/shard_map/all_to_all | solution.py:95
  226.6 1.3 copy-done
  227.9 5.4 %all-to-all-start.2 = ((f32[64,16,512]{2,1,0:T(8,128)}), f32[64,16,512]{2,1,0:T(8,128)S(1)}, u32[]{:S(2)}, u32[]{:S(2)}) async-start(f32[64,16,512]{2,1,0:T(8,128)} %all_to_all.100), calls=%async_computation.2 | async-start | bytes 4194304 | tf_op jit(solution)/shard_map/all_to_all | solution.py:85
  233.3 0.3 reduce-scatter.3.cloned.1.call-start
  233.6 2.2 fusion.26
  235.8 4.2 %copy.68 = f32[16,64,512]{2,1,0:T(8,128)} copy(f32[16,64,512]{2,0,1:T(8,128)} %bitcast.92) | data formatting | bytes 4194304 | tf_op jit(solution)/shard_map/all_to_all | solution.py:95
  239.9 2.6 reshape.194
  242.5 2.6 fusion.5
  245.2 0.9 copy.69
  246.1 38.5 %all-to-all-done.2 = f32[64,16,512]{2,1,0:T(8,128)S(1)} async-done(((f32[64,16,512]{2,1,0:T(8,128)}), f32[64,16,512]{2,1,0:T(8,128)S(1)}, u32[]{:S(2)}, u32[]{:S(2)}) %all-to-all-start.2) | async-done | bytes 2097184 | tf_op jit(solution)/shard_map/all_to_all | solution.py:85
  284.6 3.4 %all-to-all-start.7 = ((bf16[16,8,1024]{2,0,1:T(8,128)(2,1)}), bf16[16,8,1024]{2,0,1:T(8,128)(2,1)S(1)}, u32[]{:S(2)}, u32[]{:S(2)}) async-start(bf16[16,8,1024]{2,0,1:T(8,128)(2,1)} %copy.69), calls=%async_computation.7 | async-start | bytes 524288 | tf_op jit(solution)/shard_map/all_to_all | solution.py:96
  288.1 2.4 convolution_bitcast_fusion.4
  290.5 2.5 copy.59
  293.1 1.6 reshape.190
  294.7 0.9 fusion.4
  295.7 0.9 copy.60
  296.6 2.2 all-to-all-done.7
  298.7 4.9 %all-to-all-start.3 = ((bf16[16,8,1024]{2,0,1:T(8,128)(2,1)}), bf16[16,8,1024]{2,0,1:T(8,128)(2,1)S(1)}, u32[]{:S(2)}, u32[]{:S(2)}) async-start(bf16[16,8,1024]{2,0,1:T(8,128)(2,1)} %copy.60), calls=%async_computation.3 | async-start | bytes 524288 | tf_op jit(solution)/shard_map/all_to_all | solution.py:86
  303.7 25.9 %reduce-scatter.5.cloned.1.call-done = f32[2,2,16,128]{3,2,1,0:T(8,128)} async-done(((f32[2,2,128,128]{3,2,1,0:T(8,128)}), f32[2,2,16,128]{3,2,1,0:T(8,128)}) %reduce-scatter.5.cloned.1.call-update) | async-done | bytes 32784 | tf_op jit(solution)/shard_map/reduce_scatter | solution.py:105
  329.6 1.5 select_convert_fusion
  331.1 0.7 copy.94
  331.8 0.7 copy.95
  (37 shorter events, 0.9 us)
Async XLA Ops:
  7.2 48.8 %all-to-all-start = ((bf16[8,16,1024]{2,1,0:T(8,128)(2,1)}), bf16[8,16,1024]{2,1,0:T(8,128)(2,1)S(1)}, u32[]{:S(2)}, u32[]{:S(2)}) async-start(bf16[8,16,1024]{2,1,0:T(8,128)(2,1)} %bitcast.100), calls=%async_computation | async-start | bytes 524288 | tf_op jit(solution)/shard_map/all_to_all | solution.py:59
  56.0 19.8 %all-to-all-start.4 = ((bf16[8,16,1024]{2,1,0:T(8,128)(2,1)}), bf16[8,16,1024]{2,1,0:T(8,128)(2,1)S(1)}, u32[]{:S(2)}, u32[]{:S(2)}) async-start(bf16[8,16,1024]{2,1,0:T(8,128)(2,1)} %bitcast.101), calls=%async_computation.4 | async-start | bytes 524288 | tf_op jit(solution)/shard_map/all_to_all | solution.py:60
  81.5 37.2 %all-to-all-start.1 = ((bf16[16,64,512]{2,0,1:T(8,128)(2,1)}), bf16[16,64,512]{2,0,1:T(8,128)(2,1)S(1)}, u32[]{:S(2)}, u32[]{:S(2)}) async-start(bf16[16,64,512]{2,0,1:T(8,128)(2,1)} %copy.53), calls=%async_computation.1 | async-start | bytes 2097152 | tf_op jit(solution)/shard_map/all_to_all | solution.py:63
  90.8 33.7 %copy-start.7 = (s32[8192,16]{0,1:T(8,128)S(1)}, s32[8192,16]{0,1:T(8,128)}, u32[]{:S(2)}) copy-start(s32[8192,16]{0,1:T(8,128)} %param.15) | copy-start | bytes 1572868
  118.6 34.6 %all-to-all-start.5 = ((bf16[16,64,512]{2,0,1:T(8,128)(2,1)}), bf16[16,64,512]{2,0,1:T(8,128)(2,1)}, u32[]{:S(2)}, u32[]{:S(2)}) async-start(bf16[16,64,512]{2,0,1:T(8,128)(2,1)} %copy.64), calls=%async_computation.5 | async-start | bytes 2097152 | tf_op jit(solution)/shard_map/all_to_all | solution.py:64
  131.3 1.1 copy-start.10
  132.4 27.2 %copy-start.3 = (s32[256,1024]{1,0:T(8,128)}, s32[256,1024]{1,0:T(8,128)S(1)}, u32[]{:S(2)}) copy-start(s32[256,1024]{1,0:T(8,128)S(1)} %gather_fusion) | copy-start | bytes 3145732
  153.2 5.9 %copy-start.8 = (bf16[2,2,128,128]{3,2,1,0:T(8,128)(2,1)S(1)}, bf16[2,2,128,128]{3,2,1,0:T(8,128)(2,1)}, u32[]{:S(2)}) copy-start(bf16[2,2,128,128]{3,2,1,0:T(8,128)(2,1)} %param.11) | copy-start | bytes 393220
  155.4 4.2 %copy-start.9 = (bf16[2,2,128,128]{3,2,1,0:T(8,128)(2,1)S(1)}, bf16[2,2,128,128]{3,2,1,0:T(8,128)(2,1)}, u32[]{:S(2)}) copy-start(bf16[2,2,128,128]{3,2,1,0:T(8,128)(2,1)} %param.12) | copy-start | bytes 393220
  159.1 1.2 copy-start.4
  159.6 1.6 copy-start.5
  161.2 0.9 copy-start.6
  169.7 56.9 %all-to-all-start.6 = ((f32[64,16,512]{2,1,0:T(8,128)}), f32[64,16,512]{2,1,0:T(8,128)S(1)}, u32[]{:S(2)}, u32[]{:S(2)}) async-start(f32[64,16,512]{2,1,0:T(8,128)} %all_to_all.112), calls=%async_computation.6 | async-start | bytes 4194304 | tf_op jit(solution)/shard_map/all_to_all | solution.py:95
  177.3 0.8 copy-start.1
  226.6 1.3 copy-start
  227.9 56.7 %all-to-all-start.2 = ((f32[64,16,512]{2,1,0:T(8,128)}), f32[64,16,512]{2,1,0:T(8,128)S(1)}, u32[]{:S(2)}, u32[]{:S(2)}) async-start(f32[64,16,512]{2,1,0:T(8,128)} %all_to_all.100), calls=%async_computation.2 | async-start | bytes 4194304 | tf_op jit(solution)/shard_map/all_to_all | solution.py:85
  233.3 70.4 %reduce-scatter.3.cloned.1.call-start = ((), (), s32[]{:S(2)}) async-start(), calls=%async_computation.10 | async-start | bytes 294912 | tf_op jit(solution)/shard_map/reduce_scatter | solution.py:104
  242.5 45.5 %copy-start.2 = (bf16[1024,2,128,1]{0,2,3,1:T(8,128)(2,1)S(1)}, bf16[1024,2,128,1]{0,2,3,1:T(8,128)(2,1)}, u32[]{:S(2)}) copy-start(bf16[1024,2,128,1]{0,2,3,1:T(8,128)(2,1)} %copy-done.1) | copy-start | bytes 1572868
  284.6 14.2 %all-to-all-start.7 = ((bf16[16,8,1024]{2,0,1:T(8,128)(2,1)}), bf16[16,8,1024]{2,0,1:T(8,128)(2,1)S(1)}, u32[]{:S(2)}, u32[]{:S(2)}) async-start(bf16[16,8,1024]{2,0,1:T(8,128)(2,1)} %copy.69), calls=%async_computation.7 | async-start | bytes 524288 | tf_op jit(solution)/shard_map/all_to_all | solution.py:96
  288.0 41.6 %reduce-scatter.5.cloned.1.call-start = ((), (), s32[]{:S(2)}) async-start(), calls=%async_computation.11 | async-start | bytes 294912 | tf_op jit(solution)/shard_map/reduce_scatter | solution.py:105
  298.7 32.3 %all-to-all-start.3 = ((bf16[16,8,1024]{2,0,1:T(8,128)(2,1)}), bf16[16,8,1024]{2,0,1:T(8,128)(2,1)S(1)}, u32[]{:S(2)}, u32[]{:S(2)}) async-start(bf16[16,8,1024]{2,0,1:T(8,128)(2,1)} %copy.60), calls=%async_computation.3 | async-start | bytes 524288 | tf_op jit(solution)/shard_map/all_to_all | solution.py:86
Sparse Core Ops, SparseCore 0:
  236.9 35.9 reduce-scatter.2
  291.9 37.7 reduce-scatter.4
where the time goes:
time: 341 us; the launch traced here: 339 us
  waiting for transfers between devices  161 us (47%)
  local copies, waits for them, and re-layouts  56.9 us (17%)
  starting transfers between devices  51.4 us (15%)
  blocking collectives  38.4 us (11%)
  between operations  14.4 us (4%)
  matrix products  13 us (4%)
  other arithmetic  4.48 us (1%)
    all_to_all x1, waiting for transfers between devices, per_device(): lax.all_to_all(in_part, 'blk', split_axis=0, concat_axis=1, tiled=True)  38.6 us
    all_to_all x1, waiting for transfers between devices, per_device(): lax.all_to_all(out_part, 'blk', split_axis=0, concat_axis=1, tiled=True)  38.5 us
    all_gather x1, blocking collectives, per_device(): owner_rows = lax.all_gather(up_rows, 'blk', axis=0, tiled=True)  38.4 us
    all_to_all x1, waiting for transfers between devices, per_device(): lax.all_to_all(select_tiles(in_rows), 'blk', split_axis=1, concat_axis=0,...  26.3 us
    reduce_scatter x1, waiting for transfers between devices, per_device(): lax.psum_scatter(down_sum, 'tp', scatter_dimension=2, tiled=True)  25.9 us
    all_to_all x1, waiting for transfers between devices, per_device(): lax.all_to_all(select_tiles(out_rows), 'blk', split_axis=1, concat_axis=0...  17 us
    all_to_all x1, waiting for transfers between devices, per_device(): lax.all_to_all(grad_out, 'tp', split_axis=0, concat_axis=1, tiled=True)  12.1 us
    all_to_all x1, starting transfers between devices, per_device(): lax.all_to_all(inputs, 'tp', split_axis=0, concat_axis=1, tiled=True)  10.3 us
  transfers between devices with their start and end apart: 10, of which 7 were waited for; matrix products, arithmetic and copies ran while one was open for 13% of the time, Pallas kernels for 0%

commit v1 on v0

--- a/solution.py
+++ b/solution.py
@@ -42,7 +42,11 @@
     live_tiles = live[:, :, None, None]
     up_live = jnp.where(live_tiles, w_up, jnp.zeros((), jnp.bfloat16))
     down_live = jnp.where(live_tiles, w_down, jnp.zeros((), jnp.bfloat16))
-    owner_rows = lax.all_gather(up_rows, "blk", axis=0, tiled=True)
+    size = lax.axis_size("blk")
+    repeats = [size if d == 0 else 1 for d in range(up_rows.ndim)]
+    owner_rows = lax.all_to_all(
+        jnp.tile(up_rows, repeats), "blk", split_axis=0, concat_axis=0, tiled=True
+    )
     flat_owner = owner_rows.reshape(-1)
 
     def select_tiles(rows_full):

time: 341 us -> 327 us (0.959)
  blocking collectives: 38.4 us -> 18.4 us
  waiting for transfers between devices: 161 us -> 171 us
  starting transfers between devices: 51.4 us -> 45.8 us
    all_gather x1 -> x0, blocking collectives: 38.4 us -> none  [per_device(): owner_rows = lax.all_gather(up_rows, 'blk', axis=0, tiled=True)]
    all_to_all x0 -> x1, blocking collectives: none -> 18.4 us  [per_device(): lax.all_to_all(jnp.tile(up_rows, repeats), 'blk', split_axis=0, concat_ax...]
    all_to_all x1, waiting for transfers between devices: 0.01 us -> 12 us  [per_device(): lax.all_to_all(inputs, 'tp', split_axis=0, concat_axis=1, tiled=True)]
    all_to_all x1, starting transfers between devices: 7.22 us -> 3.41 us  [per_device(): lax.all_to_all(grad_out, 'tp', split_axis=0, concat_axis=1, tiled=True)]
  transfers between devices with their start and end apart: 10 -> 10, of which waited for: 7 -> 8; matrix products, arithmetic and copies ran while one was open for 13% -> 14% of each run, Pallas kernels for 0% -> 0%
where the time goes in v1:
time: 327 us; the launch traced here: 325 us
  waiting for transfers between devices  171 us (52%)
  local copies, waits for them, and re-layouts  57.6 us (18%)
  starting transfers between devices  45.8 us (14%)
  blocking collectives  18.4 us (6%)
  between operations  14.4 us (4%)
  matrix products  13 us (4%)
  other arithmetic  4.48 us (1%)
    all_to_all x1, waiting for transfers between devices, per_device(): lax.all_to_all(in_part, 'blk', split_axis=0, concat_axis=1, tiled=True)  38.6 us
    all_to_all x1, waiting for transfers between devices, per_device(): lax.all_to_all(out_part, 'blk', split_axis=0, concat_axis=1, tiled=True)  38.5 us
    all_to_all x1, waiting for transfers between devices, per_device(): lax.all_to_all(select_tiles(in_rows), 'blk', split_axis=1, concat_axis=0,...  26.4 us
    reduce_scatter x1, waiting for transfers between devices, per_device(): lax.psum_scatter(down_sum, 'tp', scatter_dimension=2, tiled=True)  25.9 us
    all_to_all x1, blocking collectives, per_device(): lax.all_to_all(jnp.tile(up_rows, repeats), 'blk', split_axis=0, concat_ax...  18.4 us
    all_to_all x1, waiting for transfers between devices, per_device(): lax.all_to_all(select_tiles(out_rows), 'blk', split_axis=1, concat_axis=0...  17 us
    all_to_all x1, waiting for transfers between devices, per_device(): lax.all_to_all(inputs, 'tp', split_axis=0, concat_axis=1, tiled=True)  12 us
    all_to_all x1, waiting for transfers between devices, per_device(): lax.all_to_all(grad_out, 'tp', split_axis=0, concat_axis=1, tiled=True)  10.4 us
  transfers between devices with their start and end apart: 10, of which 8 were waited for; matrix products, arithmetic and copies ran while one was open for 14% of the time, Pallas kernels for 0%

profile of v1, /device:TPU:6, one launch (start us, length us, event | category | flops | bytes accessed | tf_op | source)
XLA Modules:
  0.0 324.9 jit_solution(4160732199860663876)
XLA Ops:
  7.2 0.7 tile.2
  7.9 18.4 %all_to_all.132 = s32[64,2,2]{2,1,0:T(2,128)S(1)} all-to-all(s32[64,2,2]{2,1,0:T(2,128)S(1)} %tile.2), channel_id=1, replica_groups=mesh['blk'=64,'tp'=8] {'blk'}, dimensions={0} | all-to-all | bytes 2048 | tf_op jit(solution)/shard_map/all_to_all | solution.py:47
  26.3 10.3 %all-to-all-start.1 = ((bf16[8,16,1024]{2,1,0:T(8,128)(2,1)}), bf16[8,16,1024]{2,1,0:T(8,128)(2,1)S(1)}, u32[]{:S(2)}, u32[]{:S(2)}) async-start(bf16[8,16,1024]{2,1,0:T(8,128)(2,1)} %bitcast.99), calls=%async_computation.1 | async-start | bytes 524288 | tf_op jit(solution)/shard_map/all_to_all | solution.py:63
  36.8 12.0 %all-to-all-done.1 = bf16[8,16,1024]{2,1,0:T(8,128)(2,1)S(1)} async-done(((bf16[8,16,1024]{2,1,0:T(8,128)(2,1)}), bf16[8,16,1024]{2,1,0:T(8,128)(2,1)S(1)}, u32[]{:S(2)}, u32[]{:S(2)}) %all-to-all-start.1) | async-done | bytes 262176 | tf_op jit(solution)/shard_map/all_to_all | solution.py:63
  48.8 3.4 %all-to-all-start.5 = ((bf16[8,16,1024]{2,1,0:T(8,128)(2,1)}), bf16[8,16,1024]{2,1,0:T(8,128)(2,1)S(1)}, u32[]{:S(2)}, u32[]{:S(2)}) async-start(bf16[8,16,1024]{2,1,0:T(8,128)(2,1)} %bitcast.100), calls=%async_computation.5 | async-start | bytes 524288 | tf_op jit(solution)/shard_map/all_to_all | solution.py:64
  52.5 0.2 copy.51
  52.7 10.4 %all-to-all-done.5 = bf16[8,16,1024]{2,1,0:T(8,128)(2,1)S(1)} async-done(((bf16[8,16,1024]{2,1,0:T(8,128)(2,1)}), bf16[8,16,1024]{2,1,0:T(8,128)(2,1)S(1)}, u32[]{:S(2)}, u32[]{:S(2)}) %all-to-all-start.5) | async-done | bytes 262176 | tf_op jit(solution)/shard_map/all_to_all | solution.py:64
  63.4 0.2 copy.62
  63.5 0.8 gather_fusion.1
  64.4 0.8 gather_fusion.2
  65.2 0.9 select_bitcast_fusion
  66.2 0.3 copy.52
  66.5 0.7 reshape.195
  67.1 1.6 copy.53
  68.7 6.6 %all-to-all-start.2 = ((bf16[16,64,512]{2,0,1:T(8,128)(2,1)}), bf16[16,64,512]{2,0,1:T(8,128)(2,1)S(1)}, u32[]{:S(2)}, u32[]{:S(2)}) async-start(bf16[16,64,512]{2,0,1:T(8,128)(2,1)} %copy.53), calls=%async_computation.2 | async-start | bytes 2097152 | tf_op jit(solution)/shard_map/all_to_all | solution.py:67
  75.3 0.3 copy.63
  75.6 0.7 reshape.201
  76.3 1.5 copy.64
  77.8 26.4 %all-to-all-done.2 = bf16[16,64,512]{2,0,1:T(8,128)(2,1)S(1)} async-done(((bf16[16,64,512]{2,0,1:T(8,128)(2,1)}), bf16[16,64,512]{2,0,1:T(8,128)(2,1)S(1)}, u32[]{:S(2)}, u32[]{:S(2)}) %all-to-all-start.2) | async-done | bytes 1048608 | tf_op jit(solution)/shard_map/all_to_all | solution.py:67
  104.2 5.8 %all-to-all-start.6 = ((bf16[16,64,512]{2,0,1:T(8,128)(2,1)}), bf16[16,64,512]{2,0,1:T(8,128)(2,1)}, u32[]{:S(2)}, u32[]{:S(2)}) async-start(bf16[16,64,512]{2,0,1:T(8,128)(2,1)} %copy.64), calls=%async_computation.6 | async-start | bytes 2097152 | tf_op jit(solution)/shard_map/all_to_all | solution.py:68
  110.1 2.8 reshape.197
  112.8 3.7 %dynamic-slice_reduce_fusion = s32[64,16,16]{1,0,2:T(8,128)S(1)} fusion(s32[64,8,16,16]{2,1,0,3:T(8,128)} %reshape.197, s32[]{:T(128)S(6)} %select_n.78), kind=kLoop, calls=%fused_computation.27 | loop fusion | bytes 131076 | tf_op jit(solution)/shard_map/jit(dynamic_index_in_dim)/dynamic_slice | solution.py:74
  116.6 0.3 reshape.198
  116.9 1.1 gather_fusion
  118.1 1.2 reshape.196
  119.3 2.4 copy.70
  121.7 17.0 %all-to-all-done.6 = bf16[16,64,512]{2,0,1:T(8,128)(2,1)} async-done(((bf16[16,64,512]{2,0,1:T(8,128)(2,1)}), bf16[16,64,512]{2,0,1:T(8,128)(2,1)}, u32[]{:S(2)}, u32[]{:S(2)}) %all-to-all-start.6) | async-done | bytes 1048608 | tf_op jit(solution)/shard_map/all_to_all | solution.py:68
  138.8 2.2 reshape.202
  141.0 3.7 %copy.72 = bf16[1024,2,2,128]{0,3,2,1:T(8,128)(2,1)} copy(bf16[1024,2,2,128]{3,2,1,0:T(2,128)(2,1)} %reshape.202) | data formatting | bytes 2097152 | tf_op jit(solution)/shard_map/reshape | solution.py:57
  144.7 0.4 convolution_bitcast_fusion.3
  145.2 0.8 copy-done.4
  145.9 0.8 fusion.3
  146.8 0.9 copy-done.6
  147.6 1.8 convolution_bitcast_fusion
  149.4 3.1 copy.67
  152.6 2.7 all_to_all.117
  155.2 5.6 %all-to-all-start.7 = ((f32[64,16,512]{2,1,0:T(8,128)}), f32[64,16,512]{2,1,0:T(8,128)S(1)}, u32[]{:S(2)}, u32[]{:S(2)}) async-start(f32[64,16,512]{2,1,0:T(8,128)} %all_to_all.117), calls=%async_computation.7 | async-start | bytes 4194304 | tf_op jit(solution)/shard_map/all_to_all | solution.py:99
  160.9 2.0 fusion.10
  162.8 0.8 copy-done.1
  163.6 1.9 convolution_bitcast_fusion.1
  165.5 4.1 %copy.58 = f32[1024,2,2,128]{3,2,1,0:T(2,128)} copy(f32[1024,2,2,128]{0,3,2,1:T(8,128)} %convolution_bitcast_fusion.1) | data formatting | bytes 4194304 | tf_op jit(solution)/shard_map/ncj,ckjl->nckl/transpose | solution.py:86
  169.6 3.9 %all_to_all.105 = f32[64,16,512]{2,1,0:T(8,128)} reshape(f32[1024,2,2,128]{3,2,1,0:T(2,128)} %copy.58) | data formatting | bytes 4194304 | tf_op jit(solution)/shard_map/all_to_all | solution.py:89
  173.5 38.6 %all-to-all-done.7 = f32[64,16,512]{2,1,0:T(8,128)S(1)} async-done(((f32[64,16,512]{2,1,0:T(8,128)}), f32[64,16,512]{2,1,0:T(8,128)S(1)}, u32[]{:S(2)}, u32[]{:S(2)}) %all-to-all-start.7) | async-done | bytes 2097184 | tf_op jit(solution)/shard_map/all_to_all | solution.py:99
  212.2 1.3 copy-done
  213.5 5.4 %all-to-all-start.3 = ((f32[64,16,512]{2,1,0:T(8,128)}), f32[64,16,512]{2,1,0:T(8,128)S(1)}, u32[]{:S(2)}, u32[]{:S(2)}) async-start(f32[64,16,512]{2,1,0:T(8,128)} %all_to_all.105), calls=%async_computation.3 | async-start | bytes 4194304 | tf_op jit(solution)/shard_map/all_to_all | solution.py:89
  218.9 0.3 reduce-scatter.3.cloned.1.call-start
  219.1 2.2 fusion.26
  221.3 4.2 %copy.68 = f32[16,64,512]{2,1,0:T(8,128)} copy(f32[16,64,512]{2,0,1:T(8,128)} %bitcast.91) | data formatting | bytes 4194304 | tf_op jit(solution)/shard_map/all_to_all | solution.py:99
  225.5 2.6 reshape.203
  228.1 2.6 fusion.5
  230.8 0.9 copy.69
  231.6 38.5 %all-to-all-done.3 = f32[64,16,512]{2,1,0:T(8,128)S(1)} async-done(((f32[64,16,512]{2,1,0:T(8,128)}), f32[64,16,512]{2,1,0:T(8,128)S(1)}, u32[]{:S(2)}, u32[]{:S(2)}) %all-to-all-start.3) | async-done | bytes 2097184 | tf_op jit(solution)/shard_map/all_to_all | solution.py:89
  270.2 3.4 %all-to-all-start.8 = ((bf16[16,8,1024]{2,0,1:T(8,128)(2,1)}), bf16[16,8,1024]{2,0,1:T(8,128)(2,1)S(1)}, u32[]{:S(2)}, u32[]{:S(2)}) async-start(bf16[16,8,1024]{2,0,1:T(8,128)(2,1)} %copy.69), calls=%async_computation.8 | async-start | bytes 524288 | tf_op jit(solution)/shard_map/all_to_all | solution.py:100
  273.6 2.4 convolution_bitcast_fusion.4
  276.1 2.5 copy.59
  278.6 1.6 reshape.199
  280.3 0.9 fusion.4
  281.3 0.9 copy.60
  282.2 2.2 all-to-all-done.8
  284.3 4.9 %all-to-all-start.4 = ((bf16[16,8,1024]{2,0,1:T(8,128)(2,1)}), bf16[16,8,1024]{2,0,1:T(8,128)(2,1)S(1)}, u32[]{:S(2)}, u32[]{:S(2)}) async-start(bf16[16,8,1024]{2,0,1:T(8,128)(2,1)} %copy.60), calls=%async_computation.4 | async-start | bytes 524288 | tf_op jit(solution)/shard_map/all_to_all | solution.py:90
  289.3 25.9 %reduce-scatter.5.cloned.1.call-done = f32[2,2,16,128]{3,2,1,0:T(8,128)} async-done(((f32[2,2,128,128]{3,2,1,0:T(8,128)}), f32[2,2,16,128]{3,2,1,0:T(8,128)}) %reduce-scatter.5.cloned.1.call-update) | async-done | bytes 32784 | tf_op jit(solution)/shard_map/reduce_scatter | solution.py:109
  315.2 1.5 select_convert_fusion
  316.7 0.7 copy.94
  317.4 0.7 copy.95
  (38 shorter events, 1.2 us)
Async XLA Ops:
  26.3 22.5 %all-to-all-start.1 = ((bf16[8,16,1024]{2,1,0:T(8,128)(2,1)}), bf16[8,16,1024]{2,1,0:T(8,128)(2,1)S(1)}, u32[]{:S(2)}, u32[]{:S(2)}) async-start(bf16[8,16,1024]{2,1,0:T(8,128)(2,1)} %bitcast.99), calls=%async_computation.1 | async-start | bytes 524288 | tf_op jit(solution)/shard_map/all_to_all | solution.py:63
  48.8 14.3 %all-to-all-start.5 = ((bf16[8,16,1024]{2,1,0:T(8,128)(2,1)}), bf16[8,16,1024]{2,1,0:T(8,128)(2,1)S(1)}, u32[]{:S(2)}, u32[]{:S(2)}) async-start(bf16[8,16,1024]{2,1,0:T(8,128)(2,1)} %bitcast.100), calls=%async_computation.5 | async-start | bytes 524288 | tf_op jit(solution)/shard_map/all_to_all | solution.py:64
  68.7 35.5 %all-to-all-start.2 = ((bf16[16,64,512]{2,0,1:T(8,128)(2,1)}), bf16[16,64,512]{2,0,1:T(8,128)(2,1)S(1)}, u32[]{:S(2)}, u32[]{:S(2)}) async-start(bf16[16,64,512]{2,0,1:T(8,128)(2,1)} %copy.53), calls=%async_computation.2 | async-start | bytes 2097152 | tf_op jit(solution)/shard_map/all_to_all | solution.py:67
  76.3 33.8 %copy-start.7 = (s32[8192,16]{0,1:T(8,128)S(1)}, s32[8192,16]{0,1:T(8,128)}, u32[]{:S(2)}) copy-start(s32[8192,16]{0,1:T(8,128)} %param.15) | copy-start | bytes 1572868
  104.2 34.6 %all-to-all-start.6 = ((bf16[16,64,512]{2,0,1:T(8,128)(2,1)}), bf16[16,64,512]{2,0,1:T(8,128)(2,1)}, u32[]{:S(2)}, u32[]{:S(2)}) async-start(bf16[16,64,512]{2,0,1:T(8,128)(2,1)} %copy.64), calls=%async_computation.6 | async-start | bytes 2097152 | tf_op jit(solution)/shard_map/all_to_all | solution.py:68
  116.9 1.1 copy-start.10
  118.0 27.2 %copy-start.3 = (s32[256,1024]{1,0:T(8,128)}, s32[256,1024]{1,0:T(8,128)S(1)}, u32[]{:S(2)}) copy-start(s32[256,1024]{1,0:T(8,128)S(1)} %gather_fusion) | copy-start | bytes 3145732
  138.8 5.9 %copy-start.8 = (bf16[2,2,128,128]{3,2,1,0:T(8,128)(2,1)S(1)}, bf16[2,2,128,128]{3,2,1,0:T(8,128)(2,1)}, u32[]{:S(2)}) copy-start(bf16[2,2,128,128]{3,2,1,0:T(8,128)(2,1)} %param.11) | copy-start | bytes 393220
  141.0 4.2 %copy-start.9 = (bf16[2,2,128,128]{3,2,1,0:T(8,128)(2,1)S(1)}, bf16[2,2,128,128]{3,2,1,0:T(8,128)(2,1)}, u32[]{:S(2)}) copy-start(bf16[2,2,128,128]{3,2,1,0:T(8,128)(2,1)} %param.12) | copy-start | bytes 393220
  144.7 1.2 copy-start.4
  145.1 1.6 copy-start.5
  146.8 0.9 copy-start.6
  155.2 56.9 %all-to-all-start.7 = ((f32[64,16,512]{2,1,0:T(8,128)}), f32[64,16,512]{2,1,0:T(8,128)S(1)}, u32[]{:S(2)}, u32[]{:S(2)}) async-start(f32[64,16,512]{2,1,0:T(8,128)} %all_to_all.117), calls=%async_computation.7 | async-start | bytes 4194304 | tf_op jit(solution)/shard_map/all_to_all | solution.py:99
  162.8 0.8 copy-start.1
  212.2 1.3 copy-start
  213.5 56.7 %all-to-all-start.3 = ((f32[64,16,512]{2,1,0:T(8,128)}), f32[64,16,512]{2,1,0:T(8,128)S(1)}, u32[]{:S(2)}, u32[]{:S(2)}) async-start(f32[64,16,512]{2,1,0:T(8,128)} %all_to_all.105), calls=%async_computation.3 | async-start | bytes 4194304 | tf_op jit(solution)/shard_map/all_to_all | solution.py:89
  218.9 70.4 %reduce-scatter.3.cloned.1.call-start = ((), (), s32[]{:S(2)}) async-start(), calls=%async_computation.11 | async-start | bytes 294912 | tf_op jit(solution)/shard_map/reduce_scatter | solution.py:108
  228.1 45.5 %copy-start.2 = (bf16[1024,2,128,1]{0,2,3,1:T(8,128)(2,1)S(1)}, bf16[1024,2,128,1]{0,2,3,1:T(8,128)(2,1)}, u32[]{:S(2)}) copy-start(bf16[1024,2,128,1]{0,2,3,1:T(8,128)(2,1)} %copy-done.1) | copy-start | bytes 1572868
  270.2 14.2 %all-to-all-start.8 = ((bf16[16,8,1024]{2,0,1:T(8,128)(2,1)}), bf16[16,8,1024]{2,0,1:T(8,128)(2,1)S(1)}, u32[]{:S(2)}, u32[]{:S(2)}) async-start(bf16[16,8,1024]{2,0,1:T(8,128)(2,1)} %copy.69), calls=%async_computation.8 | async-start | bytes 524288 | tf_op jit(solution)/shard_map/all_to_all | solution.py:100
  273.6 41.6 %reduce-scatter.5.cloned.1.call-start = ((), (), s32[]{:S(2)}) async-start(), calls=%async_computation.12 | async-start | bytes 294912 | tf_op jit(solution)/shard_map/reduce_scatter | solution.py:109
  284.3 32.3 %all-to-all-start.4 = ((bf16[16,8,1024]{2,0,1:T(8,128)(2,1)}), bf16[16,8,1024]{2,0,1:T(8,128)(2,1)S(1)}, u32[]{:S(2)}, u32[]{:S(2)}) async-start(bf16[16,8,1024]{2,0,1:T(8,128)(2,1)} %copy.60), calls=%async_computation.4 | async-start | bytes 524288 | tf_op jit(solution)/shard_map/all_to_all | solution.py:90
Sparse Core Ops, SparseCore 0:
  222.5 35.9 reduce-scatter.2
  277.4 37.7 reduce-scatter.4
